TPU v7x, 32 devices: a whole 2x2x4 slice. The times are simulated.
32 devices in a mesh: chan: 16 (over z, x, core), tm: 2 (over y).
Axes of the slice: x: 2, y: 2, z: 4, core: 2. Of those that a mesh axis runs over, the one named last changes fastest.
Arguments:
- raw_strain: bfloat16 [2048, 16384], P('chan', 'tm'), may hold values from -6 to 6
- fir_taps: bfloat16 [64], replicated, may hold values from -0.75 to 0.75
- sources: int32 [2, 8], replicated, may hold values from 0 to 2047, as said below
Outputs:
- correlation: float32 [2, 8, 257, 2048], P(None, 'tm', None, 'chan')
Inputs may be any that keep to these rules, and one draw needn't show every extreme that they name: `sources`: the 16 entries are distinct channel indices; the first and the last channel are always among them.
All inputs are finite; a program needn't handle non-finite values.
Results may differ from a plain program's by a relative error of at most 0.0037.
Values may be sent and summed in bfloat16 or wider, within the bound.
A program may use at most 64 MiB of HBM per device.

v0:
```python
import math

import jax
import jax.numpy as jnp
from jax import lax
from jax.sharding import PartitionSpec as P

TAPS = 64
DECIM = 4
HALF_WIN = 32
LAGS = 257
HALF_LAG = 128
STEPS = 2


tile_width = 128


def shifted(x, axis, by):
    length = lax.axis_size(axis)
    pairs = [(i, i + by) for i in range(length) if 0 <= i + by < length]
    return lax.ppermute(x, axis, pairs)


def padded_2(x, sides, width):
    for axis, dim in sides:
        size, length = (lax.axis_size(axis), x.shape[dim])
        up = [(i, (i + 1) % size) for i in range(size - 1)]
        down = [(j, i) for i, j in up]
        last = lax.slice_in_dim(x, length - width, length, axis=dim)
        initial = lax.slice_in_dim(x, 0, width, axis=dim)
        before = lax.ppermute(last, axis, up)
        after = lax.ppermute(initial, axis, down)
        x = jnp.concatenate([before, x, after], axis=dim)
    return x


def filter_matrix(fir_taps, phases, guard_width):
    count = fir_taps.shape[0]
    offset = jnp.arange(tile_width + guard_width)[:, None, None]
    phase_ids = jnp.arange(phases)[None, :, None]
    column = jnp.arange(tile_width)[None, None, :]
    tap_index = count - phases * (offset - column) - phase_ids
    matches = tap_index[..., None] == jnp.arange(count)[None, None, None, :]
    weights = jnp.sum(jnp.where(matches, fir_taps.astype(jnp.float32), 0.0), axis=-1)
    return weights.astype(jnp.bfloat16).reshape((tile_width + guard_width) * phases, tile_width)


def decimate(extended, fir_taps, outputs):
    phases = DECIM
    guard_width = TAPS // DECIM
    channel_count = extended.shape[0]
    block_count = outputs // tile_width
    polyphase = extended.reshape(channel_count, outputs + guard_width, phases)
    padded = jnp.pad(polyphase, ((0, 0), (0, tile_width - guard_width), (0, 0)))
    leading = padded[:, :outputs].reshape(channel_count, block_count, tile_width, phases)
    trailing = padded[:, tile_width : tile_width + outputs].reshape(
        channel_count, block_count, tile_width, phases
    )
    blocks = jnp.concatenate([leading, trailing[:, :, :guard_width]], axis=2)
    blocks = blocks.reshape(channel_count, block_count, (tile_width + guard_width) * phases)
    result = jnp.einsum(
        "cbj,ji->cbi",
        blocks,
        filter_matrix(fir_taps, phases, guard_width),
        preferred_element_type=jnp.float32,
    )
    return result.reshape(channel_count, outputs)


def window_sums(magnitude, outputs):
    span_width = 2 * HALF_WIN
    channel_count = magnitude.shape[0]
    block_count = outputs // tile_width
    padded = jnp.pad(magnitude, ((0, 0), (0, tile_width - span_width)))
    leading = padded[:, :outputs].reshape(channel_count, block_count, tile_width)
    trailing = padded[:, tile_width : tile_width + outputs].reshape(
        channel_count, block_count, tile_width
    )
    blocks = jnp.concatenate([leading, trailing[:, :, :span_width]], axis=2)
    row_ids = jnp.arange(tile_width + span_width)[:, None]
    col_ids = jnp.arange(tile_width)[None, :]
    band = ((row_ids >= col_ids) & (row_ids <= col_ids + span_width)).astype(jnp.float32)
    sums = jnp.einsum(
        "cbj,ji->cbi",
        blocks,
        band,
        precision=lax.Precision.HIGHEST,
        preferred_element_type=jnp.float32,
    )
    return sums.reshape(channel_count, outputs)


def lag_products(extended_traces, receivers):
    length = receivers.shape[1]
    width = length + LAGS - 1

    def single(trace):
        tiled = jnp.tile(trace, LAGS + 1)[: LAGS * (width + 1)].reshape(LAGS, width + 1)
        toeplitz = tiled[::-1, :length]
        return jnp.einsum("lm,rm->lr", toeplitz, receivers, preferred_element_type=jnp.float32)

    return lax.map(single, extended_traces)


def per_device(raw_strain, fir_taps, sources):
    dec_dev = raw_strain.shape[1] // DECIM
    left_rim = shifted(raw_strain[:, raw_strain.shape[1] - TAPS :], "tm", 1)
    decimated = decimate(jnp.concatenate([left_rim, raw_strain], axis=1), fir_taps, dec_dev)
    beside_all = padded_2(decimated, (("tm", 1),), HALF_WIN)
    magnitude = jnp.abs(beside_all)
    level = window_sums(magnitude, dec_dev) / (2 * HALF_WIN + 1) + 1e-05
    white = (decimated / level).astype(jnp.bfloat16)
    channel_count = white.shape[0]
    my_block = lax.axis_index("chan")
    owner_ids = sources // channel_count
    local_rows = sources % channel_count
    traces = []
    for step_index in range(STEPS):
        picks = (local_rows[step_index][:, None] == jnp.arange(channel_count)[None, :]) & (
            owner_ids[step_index][:, None] == my_block
        )
        summed = lax.psum(
            jnp.dot(picks.astype(jnp.bfloat16), white, preferred_element_type=jnp.float32), "chan"
        )
        traces.append(summed.astype(jnp.bfloat16))
    scale = 1.0 / math.sqrt(dec_dev * lax.axis_size("tm"))
    terms = []
    for step_index in range(STEPS):
        extended = padded_2(traces[step_index], (("tm", 1),), HALF_LAG)
        terms.append(lag_products(extended, white) * scale)
    return lax.psum_scatter(jnp.stack(terms), "tm", scatter_dimension=1, tiled=True)


def solution(mesh):
    placed = (P("chan", "tm"), P(), P())
    return jax.shard_map(
        per_device,
        mesh=mesh,
        in_specs=placed,
        out_specs=P(None, "tm", None, "chan"),
        check_vma=False,
    )
```

profile of v0, /device:TPU:0, one launch (start us, length us, event | category | flops | bytes accessed | tf_op | source)
XLA Modules:
  0.0 399.5 jit_solution(1200064050294466446)
XLA Ops:
  6.5 3.2 copy.28
  9.8 4.9 %collective-permute-start = (bf16[128,64]{0,1:T(8,128)(2,1)S(1)}, bf16[128,64]{0,1:T(8,128)(2,1)S(1)}, u32[]{:S(2)}, u32[]{:S(2)}) collective-permute-start(bf16[128,64]{0,1:T(8,128)(2,1)S(1)} %slice.86), channel_id=1, source_target_pairs={{0,1},{2,3},{4,5},{6,7},{8,9},{10,11},{12,13},{14,15},{16,17},{18,... | collective-permute-start | bytes 49160 | tf_op jit(solution)/shard_map/ppermute | solution.py:22
  14.8 6.9 %select_reduce_fusion = bf16[144,4,128]{2,1,0:T(4,128)(2,1)S(1)} fusion(f32[64]{0:T(128)S(1)} %convert_element_type.22, s32[144,4,128]{2,1,0:T(4,128)S(1)} %iota_subtract_fusion), kind=kLoop, calls=%fused_computation.4 | loop fusion | flops 14082048 | bytes 442624 | tf_op jit(solution)/shard_map/reduce_sum | solution.py:45
  22.0 2.3 fusion.32
  28.6 4.0 collective-permute-done.2
  36.9 60.9 %all-reduce.8 = (bf16[8,2048]{1,0:T(8,128)(2,1)S(1)}, bf16[8,2048]{1,0:T(8,128)(2,1)S(1)}) all-reduce(f32[8,2048]{1,0:T(8,128)S(1)} %fusion.24, f32[8,2048]{1,0:T(8,128)S(1)} %fusion.21), channel_id=1, replica_groups=mesh['chan'=16,'tm'=2] {'chan'}, use_global_device_ids=true, to_apply=%region_4.5 | all-reduce | flops 32768 | bytes 196608 | tf_op jit(solution)/shard_map/psum | solution.py:123
  101.0 4.5 %collective-permute-start.5 = (bf16[8,128]{1,0:T(8,128)(2,1)S(1)}, bf16[8,128]{1,0:T(8,128)(2,1)S(1)}, u32[]{:S(2)}, u32[]{:S(2)}) collective-permute-start(bf16[8,128]{1,0:T(8,128)(2,1)S(1)} %get-tuple-element.77), channel_id=1, source_target_pairs={{0,1},{2,3},{4,5},{6,7},{8,9},{10,11},{12,13},{14,15},{16,17},{18,... | collective-permute-start | bytes 6152 | tf_op jit(solution)/shard_map/ppermute | solution.py:32
  108.1 107.8 %while.20 = (s32[]{:T(128)}, f32[8,257,128]{2,0,1:T(8,128)}, bf16[8,2304]{1,0:T(8,128)(2,1)S(1)}, bf16[128,2048]{1,0:T(8,128)(2,1)S(1)}, s32[]{:T(128)}, /*index=5*/s32[]{:T(128)}) while((s32[]{:T(128)}, f32[8,257,128]{2,0,1:T(8,128)}, bf16[8,2304]{1,0:T(8,128)(2,1)S(1)}, bf16[128,2048]{1,0:T(8,128)(2,1)S(1)}, s32[]{:T(128)}, ...), condition=%wide.region_3.4_spmd, body=%wide.region_2.3_spmd.sunk | while | flops 134742016 | bytes 14765141 | solution.py:103
  109.7 2.1 reshape.93
  112.0 4.0 rev.8
  116.6 5.0 %dynamic_update_slice.9 = f32[8,257,128]{2,0,1:T(8,128)} dynamic-update-slice(f32[8,257,128]{2,0,1:T(8,128)} %get-tuple-element.162, f32[1,257,128]{2,0,1:T(1,128)S(1)} %copy.59, s32[]{:T(128)} %get-tuple-element.161, s32[]{:T(128)} %constant.54.clone.1..sunk, s32[]{:T(128)} %constant.54.clone.1..sunk) | dynamic-update-slice | bytes 263172 | tf_op jit(solution)/shard_map/while/body/jit(dynamic_update_index_in_dim)/dynamic_update_slice | solution.py:103
  123.2 2.1 reshape.93
  125.4 4.0 rev.8
  130.1 5.0 %dynamic_update_slice.9 = f32[8,257,128]{2,0,1:T(8,128)} dynamic-update-slice(f32[8,257,128]{2,0,1:T(8,128)} %get-tuple-element.162, f32[1,257,128]{2,0,1:T(1,128)S(1)} %copy.59, s32[]{:T(128)} %get-tuple-element.161, s32[]{:T(128)} %constant.54.clone.1..sunk, s32[]{:T(128)} %constant.54.clone.1..sunk) | dynamic-update-slice | bytes 263172 | tf_op jit(solution)/shard_map/while/body/jit(dynamic_update_index_in_dim)/dynamic_update_slice | solution.py:103
  138.9 4.0 rev.8
  143.5 5.0 %dynamic_update_slice.9 = f32[8,257,128]{2,0,1:T(8,128)} dynamic-update-slice(f32[8,257,128]{2,0,1:T(8,128)} %get-tuple-element.162, f32[1,257,128]{2,0,1:T(1,128)S(1)} %copy.59, s32[]{:T(128)} %get-tuple-element.161, s32[]{:T(128)} %constant.54.clone.1..sunk, s32[]{:T(128)} %constant.54.clone.1..sunk) | dynamic-update-slice | bytes 263172 | tf_op jit(solution)/shard_map/while/body/jit(dynamic_update_index_in_dim)/dynamic_update_slice | solution.py:103
  150.1 2.1 reshape.93
  152.4 4.0 rev.8
  157.0 5.0 %dynamic_update_slice.9 = f32[8,257,128]{2,0,1:T(8,128)} dynamic-update-slice(f32[8,257,128]{2,0,1:T(8,128)} %get-tuple-element.162, f32[1,257,128]{2,0,1:T(1,128)S(1)} %copy.59, s32[]{:T(128)} %get-tuple-element.161, s32[]{:T(128)} %constant.54.clone.1..sunk, s32[]{:T(128)} %constant.54.clone.1..sunk) | dynamic-update-slice | bytes 263172 | tf_op jit(solution)/shard_map/while/body/jit(dynamic_update_index_in_dim)/dynamic_update_slice | solution.py:103
  163.6 2.1 reshape.93
  165.9 4.0 rev.8
  170.5 5.0 %dynamic_update_slice.9 = f32[8,257,128]{2,0,1:T(8,128)} dynamic-update-slice(f32[8,257,128]{2,0,1:T(8,128)} %get-tuple-element.162, f32[1,257,128]{2,0,1:T(1,128)S(1)} %copy.59, s32[]{:T(128)} %get-tuple-element.161, s32[]{:T(128)} %constant.54.clone.1..sunk, s32[]{:T(128)} %constant.54.clone.1..sunk) | dynamic-update-slice | bytes 263172 | tf_op jit(solution)/shard_map/while/body/jit(dynamic_update_index_in_dim)/dynamic_update_slice | solution.py:103
  179.3 4.0 rev.8
  184.0 5.0 %dynamic_update_slice.9 = f32[8,257,128]{2,0,1:T(8,128)} dynamic-update-slice(f32[8,257,128]{2,0,1:T(8,128)} %get-tuple-element.162, f32[1,257,128]{2,0,1:T(1,128)S(1)} %copy.59, s32[]{:T(128)} %get-tuple-element.161, s32[]{:T(128)} %constant.54.clone.1..sunk, s32[]{:T(128)} %constant.54.clone.1..sunk) | dynamic-update-slice | bytes 263172 | tf_op jit(solution)/shard_map/while/body/jit(dynamic_update_index_in_dim)/dynamic_update_slice | solution.py:103
  192.8 4.0 rev.8
  197.4 5.0 %dynamic_update_slice.9 = f32[8,257,128]{2,0,1:T(8,128)} dynamic-update-slice(f32[8,257,128]{2,0,1:T(8,128)} %get-tuple-element.162, f32[1,257,128]{2,0,1:T(1,128)S(1)} %copy.59, s32[]{:T(128)} %get-tuple-element.161, s32[]{:T(128)} %constant.54.clone.1..sunk, s32[]{:T(128)} %constant.54.clone.1..sunk) | dynamic-update-slice | bytes 263172 | tf_op jit(solution)/shard_map/while/body/jit(dynamic_update_index_in_dim)/dynamic_update_slice | solution.py:103
  206.3 4.0 rev.8
  210.9 5.0 %dynamic_update_slice.9 = f32[8,257,128]{2,0,1:T(8,128)} dynamic-update-slice(f32[8,257,128]{2,0,1:T(8,128)} %get-tuple-element.162, f32[1,257,128]{2,0,1:T(1,128)S(1)} %copy.59, s32[]{:T(128)} %get-tuple-element.161, s32[]{:T(128)} %constant.54.clone.1..sunk, s32[]{:T(128)} %constant.54.clone.1..sunk) | dynamic-update-slice | bytes 263172 | tf_op jit(solution)/shard_map/while/body/jit(dynamic_update_index_in_dim)/dynamic_update_slice | solution.py:103
  217.0 108.1 %while.21 = (s32[]{:T(128)}, f32[8,257,128]{2,0,1:T(8,128)}, bf16[8,2304]{1,0:T(8,128)(2,1)S(1)}, bf16[128,2048]{1,0:T(8,128)(2,1)S(1)}, s32[]{:T(128)}, /*index=5*/s32[]{:T(128)}) while((s32[]{:T(128)}, f32[8,257,128]{2,0,1:T(8,128)}, bf16[8,2304]{1,0:T(8,128)(2,1)S(1)}, bf16[128,2048]{1,0:T(8,128)(2,1)S(1)}, s32[]{:T(128)}, ...), condition=%wide.region_6.7_spmd, body=%wide.region_5.6_spmd.sunk | while | flops 134742016 | bytes 14765141 | solution.py:103
  220.8 4.0 rev.9
  225.4 5.0 %dynamic_update_slice.10 = f32[8,257,128]{2,0,1:T(8,128)} dynamic-update-slice(f32[8,257,128]{2,0,1:T(8,128)} %get-tuple-element.144, f32[1,257,128]{2,0,1:T(1,128)S(1)} %copy.60, s32[]{:T(128)} %get-tuple-element.143, s32[]{:T(128)} %constant.54.clone.1..sunk.1, s32[]{:T(128)} %constant.54.clone.1..sunk.1) | dynamic-update-slice | bytes 263172 | tf_op jit(solution)/shard_map/while/body/jit(dynamic_update_index_in_dim)/dynamic_update_slice | solution.py:103
  234.3 4.0 rev.9
  238.9 5.0 %dynamic_update_slice.10 = f32[8,257,128]{2,0,1:T(8,128)} dynamic-update-slice(f32[8,257,128]{2,0,1:T(8,128)} %get-tuple-element.144, f32[1,257,128]{2,0,1:T(1,128)S(1)} %copy.60, s32[]{:T(128)} %get-tuple-element.143, s32[]{:T(128)} %constant.54.clone.1..sunk.1, s32[]{:T(128)} %constant.54.clone.1..sunk.1) | dynamic-update-slice | bytes 263172 | tf_op jit(solution)/shard_map/while/body/jit(dynamic_update_index_in_dim)/dynamic_update_slice | solution.py:103
  247.8 4.0 rev.9
  252.5 5.0 %dynamic_update_slice.10 = f32[8,257,128]{2,0,1:T(8,128)} dynamic-update-slice(f32[8,257,128]{2,0,1:T(8,128)} %get-tuple-element.144, f32[1,257,128]{2,0,1:T(1,128)S(1)} %copy.60, s32[]{:T(128)} %get-tuple-element.143, s32[]{:T(128)} %constant.54.clone.1..sunk.1, s32[]{:T(128)} %constant.54.clone.1..sunk.1) | dynamic-update-slice | bytes 263172 | tf_op jit(solution)/shard_map/while/body/jit(dynamic_update_index_in_dim)/dynamic_update_slice | solution.py:103
  261.4 4.0 rev.9
  266.0 5.0 %dynamic_update_slice.10 = f32[8,257,128]{2,0,1:T(8,128)} dynamic-update-slice(f32[8,257,128]{2,0,1:T(8,128)} %get-tuple-element.144, f32[1,257,128]{2,0,1:T(1,128)S(1)} %copy.60, s32[]{:T(128)} %get-tuple-element.143, s32[]{:T(128)} %constant.54.clone.1..sunk.1, s32[]{:T(128)} %constant.54.clone.1..sunk.1) | dynamic-update-slice | bytes 263172 | tf_op jit(solution)/shard_map/while/body/jit(dynamic_update_index_in_dim)/dynamic_update_slice | solution.py:103
  274.9 4.0 rev.9
  279.5 5.0 %dynamic_update_slice.10 = f32[8,257,128]{2,0,1:T(8,128)} dynamic-update-slice(f32[8,257,128]{2,0,1:T(8,128)} %get-tuple-element.144, f32[1,257,128]{2,0,1:T(1,128)S(1)} %copy.60, s32[]{:T(128)} %get-tuple-element.143, s32[]{:T(128)} %constant.54.clone.1..sunk.1, s32[]{:T(128)} %constant.54.clone.1..sunk.1) | dynamic-update-slice | bytes 263172 | tf_op jit(solution)/shard_map/while/body/jit(dynamic_update_index_in_dim)/dynamic_update_slice | solution.py:103
  288.4 4.0 rev.9
  293.0 5.0 %dynamic_update_slice.10 = f32[8,257,128]{2,0,1:T(8,128)} dynamic-update-slice(f32[8,257,128]{2,0,1:T(8,128)} %get-tuple-element.144, f32[1,257,128]{2,0,1:T(1,128)S(1)} %copy.60, s32[]{:T(128)} %get-tuple-element.143, s32[]{:T(128)} %constant.54.clone.1..sunk.1, s32[]{:T(128)} %constant.54.clone.1..sunk.1) | dynamic-update-slice | bytes 263172 | tf_op jit(solution)/shard_map/while/body/jit(dynamic_update_index_in_dim)/dynamic_update_slice | solution.py:103
  301.9 4.0 rev.9
  306.5 5.0 %dynamic_update_slice.10 = f32[8,257,128]{2,0,1:T(8,128)} dynamic-update-slice(f32[8,257,128]{2,0,1:T(8,128)} %get-tuple-element.144, f32[1,257,128]{2,0,1:T(1,128)S(1)} %copy.60, s32[]{:T(128)} %get-tuple-element.143, s32[]{:T(128)} %constant.54.clone.1..sunk.1, s32[]{:T(128)} %constant.54.clone.1..sunk.1) | dynamic-update-slice | bytes 263172 | tf_op jit(solution)/shard_map/while/body/jit(dynamic_update_index_in_dim)/dynamic_update_slice | solution.py:103
  313.2 2.1 reshape.94
  315.4 4.0 rev.9
  320.0 5.0 %dynamic_update_slice.10 = f32[8,257,128]{2,0,1:T(8,128)} dynamic-update-slice(f32[8,257,128]{2,0,1:T(8,128)} %get-tuple-element.144, f32[1,257,128]{2,0,1:T(1,128)S(1)} %copy.60, s32[]{:T(128)} %get-tuple-element.143, s32[]{:T(128)} %constant.54.clone.1..sunk.1, s32[]{:T(128)} %constant.54.clone.1..sunk.1) | dynamic-update-slice | bytes 263172 | tf_op jit(solution)/shard_map/while/body/jit(dynamic_update_index_in_dim)/dynamic_update_slice | solution.py:103
  330.1 59.8 %all-reduce.7.cloned.1.call-done = f32[2,8,257,128]{3,1,2,0:T(8,128)} async-done(((f32[2,8,257,128]{3,1,2,0:T(8,128)}), f32[2,8,257,128]{3,1,2,0:T(8,128)}) %all-reduce.7.cloned.1.call-update) | async-done | bytes 2105360
  389.9 2.7 constant_dynamic-slice_fusion
  (174 shorter events, 80.4 us)
Async XLA Ops:
  6.5 8.2 %copy-start.1 = (bf16[64]{0:T(256)(128)(2,1)S(1)}, bf16[64]{0:T(256)(128)(2,1)}, u32[]{:S(2)}) copy-start(bf16[64]{0:T(256)(128)(2,1)} %param.8) | copy-start | bytes 388
  6.5 8.3 %copy-start = (s32[2,8]{1,0:T(2,128)S(1)}, s32[2,8]{1,0:T(2,128)}, u32[]{:S(2)}) copy-start(s32[2,8]{1,0:T(2,128)} %param.9) | copy-start | bytes 196
  6.5 383.4 %all-reduce.7.cloned.1.call-start = ((), (), s32[]{:S(2)}) async-start(), calls=%async_computation | async-start | bytes 4210688
  9.8 12.0 %collective-permute-start = (bf16[128,64]{0,1:T(8,128)(2,1)S(1)}, bf16[128,64]{0,1:T(8,128)(2,1)S(1)}, u32[]{:S(2)}, u32[]{:S(2)}) collective-permute-start(bf16[128,64]{0,1:T(8,128)(2,1)S(1)} %slice.86), channel_id=1, source_target_pairs={{0,1},{2,3},{4,5},{6,7},{8,9},{10,11},{12,13},{14,15},{16,17},{18,... | collective-permute-start | bytes 49160 | tf_op jit(solution)/shard_map/ppermute | solution.py:22
  25.6 3.0 collective-permute-start.1
  26.9 5.6 %collective-permute-start.2 = (f32[128,32]{0,1:T(8,128)S(1)}, f32[128,32]{0,1:T(8,128)S(1)}, u32[]{:S(2)}, u32[]{:S(2)}) collective-permute-start(f32[128,32]{0,1:T(8,128)S(1)} %get-tuple-element.74), channel_id=1, source_target_pairs={{1,0},{3,2},{5,4},{7,6},{9,8},{11,10},{13,12},{15,14},{17,16},{19,... | collective-permute-start | bytes 49160 | tf_op jit(solution)/shard_map/ppermute | solution.py:33
  97.8 9.3 %collective-permute-start.3 = (bf16[8,128]{1,0:T(8,128)(2,1)S(1)}, bf16[8,128]{1,0:T(8,128)(2,1)S(1)}, u32[]{:S(2)}, u32[]{:S(2)}) collective-permute-start(bf16[8,128]{1,0:T(8,128)(2,1)S(1)} %get-tuple-element.75), channel_id=1, source_target_pairs={{0,1},{2,3},{4,5},{6,7},{8,9},{10,11},{12,13},{14,15},{16,17},{18,... | collective-permute-start | bytes 6152 | tf_op jit(solution)/shard_map/ppermute | solution.py:32
  99.7 7.4 %collective-permute-start.4 = (bf16[8,128]{1,0:T(8,128)(2,1)S(1)}, bf16[8,128]{1,0:T(8,128)(2,1)S(1)}, u32[]{:S(2)}, u32[]{:S(2)}) collective-permute-start(bf16[8,128]{1,0:T(8,128)(2,1)S(1)} %get-tuple-element.76), channel_id=1, source_target_pairs={{1,0},{3,2},{5,4},{7,6},{9,8},{11,10},{13,12},{15,14},{17,16},{19,... | collective-permute-start | bytes 6152 | tf_op jit(solution)/shard_map/ppermute | solution.py:33
  101.0 114.9 %collective-permute-start.5 = (bf16[8,128]{1,0:T(8,128)(2,1)S(1)}, bf16[8,128]{1,0:T(8,128)(2,1)S(1)}, u32[]{:S(2)}, u32[]{:S(2)}) collective-permute-start(bf16[8,128]{1,0:T(8,128)(2,1)S(1)} %get-tuple-element.77), channel_id=1, source_target_pairs={{0,1},{2,3},{4,5},{6,7},{8,9},{10,11},{12,13},{14,15},{16,17},{18,... | collective-permute-start | bytes 6152 | tf_op jit(solution)/shard_map/ppermute | solution.py:32
  105.6 110.4 %collective-permute-start.6 = (bf16[8,128]{1,0:T(8,128)(2,1)S(1)}, bf16[8,128]{1,0:T(8,128)(2,1)S(1)}, u32[]{:S(2)}, u32[]{:S(2)}) collective-permute-start(bf16[8,128]{1,0:T(8,128)(2,1)S(1)} %get-tuple-element.78), channel_id=1, source_target_pairs={{1,0},{3,2},{5,4},{7,6},{9,8},{11,10},{13,12},{15,14},{17,16},{19,... | collective-permute-start | bytes 6152 | tf_op jit(solution)/shard_map/ppermute | solution.py:33
  328.2 0.7 copy-start.2
Sparse Core Ops, SparseCore 0:
  328.4 61.4 all-reduce.6
where the time goes:
time: 402 us; the launch traced here: 399 us
  local copies, waits for them, and re-layouts  221 us (55%)
  waiting for transfers between devices  63.8 us (16%)
  blocking collectives  60.9 us (15%)
  starting transfers between devices  16.7 us (4%)
  between operations  14.4 us (4%)
  other arithmetic  11.8 us (3%)
  matrix products  9.57 us (2%)
    dynamic_update_slice x32, local copies, waits for them, and re-layouts, lag_products(): return lax.map(single, extended_traces)  82.6 us
    rev x16, local copies, waits for them, and re-layouts, single(): toeplitz = tiled[::-1, :length]  63.6 us
    psum x1, blocking collectives, per_device(): lax.psum(jnp.dot(picks.astype(jnp.bfloat16), white, preferred_element_typ...  60.9 us
    unnamed x2, waiting for transfers between devices  59.8 us
    reshape x16, local copies, waits for them, and re-layouts, single(): jnp.tile(trace, LAGS + 1)[:LAGS * (width + 1)].reshape(LAGS, width + 1)  33.7 us
    another operation x32, local copies, waits for them, and re-layouts, single(): jnp.tile(trace, LAGS + 1)[:LAGS * (width + 1)].reshape(LAGS, width + 1)  23.4 us
  transfers between devices with their start and end apart: 8, of which 2 were waited for; matrix products, arithmetic and copies ran while one was open for 29% of the time, Pallas kernels for 0%

commit v1 on v0

v1 whole, which is shorter than its diff:
```python
import functools
import math

import jax
import jax.numpy as jnp
from jax import lax
from jax.experimental import pallas as pl
from jax.experimental.pallas import tpu as pltpu
from jax.sharding import PartitionSpec as P

TAPS = 64
DECIM = 4
HALF_WIN = 32
LAGS = 257
HALF_LAG = 128
STEPS = 2
W = 128
SLAB = 8
PIECES = 4
LEFT = 256
RIGHT = 128
MESH = pl.DeviceIdType.MESH


def nt(a, b):
    return lax.dot_general(
        a, b, (((1,), (1,)), ((), ())), preferred_element_type=jnp.float32
    )


def aligned(x):
    return pl.multiple_of(x, W)


def kernel(
    C, T, scale,
    raw_ref, taps_ref, src_ref, out_ref,
    x_ref, dec_ref, hi_ref, lo_ref, white_ref, send1, recv1, recv2, gref, acc_ref,
    load_sem, halo_send, halo_recv, s1_sem, r1_sem, s2_sem, r2_sem, own_sem, bulk_send, bulk_recv,
):
    c = lax.axis_index("chan")
    t = lax.axis_index("tm")
    N = C * T
    rows, raw_len = raw_ref.shape
    dec_len = raw_len // DECIM
    nb = dec_len // W
    per_dev = (T * nb) // C
    half = nb // per_dev
    step_len = src_ref.shape[1] // T
    ns = STEPS * step_len
    me = c * T + t

    barrier = pltpu.get_barrier_semaphore()

    def greet(d, _):
        other = lax.rem(me + d, N)
        pl.semaphore_signal(
            barrier, inc=1, device_id=(other // T, lax.rem(other, T)), device_id_type=MESH
        )
        return 0

    lax.fori_loop(1, N, greet, 0)

    seg = raw_len // PIECES
    loads = []
    for i in range(PIECES):
        load = pltpu.make_async_copy(
            raw_ref.at[:, pl.ds(i * seg, seg)],
            x_ref.at[:, pl.ds(LEFT + i * seg, seg)],
            load_sem.at[i],
        )
        load.start()
        loads.append(load)

    taps = jnp.broadcast_to(taps_ref[...], (16, TAPS))
    place = lax.broadcasted_iota(jnp.int32, (TAPS, W), 1) == lax.rem(
        W - lax.broadcasted_iota(jnp.int32, (TAPS, W), 0), W
    )
    base = jnp.dot(
        taps, place.astype(jnp.float32).astype(jnp.bfloat16), preferred_element_type=jnp.float32
    )
    rolled = pltpu.roll(
        jnp.broadcast_to(base[0:1, :], (W, W)), 0, 1, stride=DECIM, stride_axis=0
    )
    row_id = lax.broadcasted_iota(jnp.int32, (W, W), 0)
    lane_id = lax.broadcasted_iota(jnp.int32, (W, W), 1)
    fts = []
    for jc in range(DECIM + 1):
        k = DECIM * row_id + W - W * jc - lane_id
        fts.append(jnp.where((k >= 0) & (k < W), rolled, 0.0).astype(jnp.bfloat16))
    ft = jnp.concatenate(fts, axis=1)

    pl.semaphore_wait(barrier, N - 1)

    to_right = pltpu.make_async_remote_copy(
        src_ref=raw_ref.at[:, pl.ds(raw_len - LEFT, LEFT)],
        dst_ref=x_ref.at[:, pl.ds(0, LEFT)],
        send_sem=halo_send.at[0], recv_sem=halo_recv.at[0],
        device_id=(c, lax.rem(t + 1, T)), device_id_type=MESH,
    )
    to_left = pltpu.make_async_remote_copy(
        src_ref=raw_ref.at[:, pl.ds(0, RIGHT)],
        dst_ref=x_ref.at[:, pl.ds(LEFT + raw_len, RIGHT)],
        send_sem=halo_send.at[1], recv_sem=halo_recv.at[1],
        device_id=(c, lax.rem(t + T - 1, T)), device_id_type=MESH,
    )

    @pl.when(t < T - 1)
    def _():
        to_right.start()

    @pl.when(t > 0)
    def _():
        to_left.start()

    @pl.when(t == 0)
    def _():
        x_ref[:, 0:LEFT] = jnp.zeros((rows, LEFT), jnp.bfloat16)

    @pl.when(t == T - 1)
    def _():
        x_ref[:, LEFT + raw_len:] = jnp.zeros((rows, RIGHT), jnp.bfloat16)

    total = T * dec_len
    white_ref[:, 0:W] = jnp.zeros((rows, W), jnp.bfloat16)
    white_ref[:, W + total:] = jnp.zeros((rows, W), jnp.bfloat16)

    def put_mag(b, d):
        mag = jnp.abs(d)
        hi = mag.astype(jnp.bfloat16)
        hi_ref[:, (b + 1) * W:(b + 2) * W] = hi
        lo_ref[:, (b + 1) * W:(b + 2) * W] = (mag - hi.astype(jnp.float32)).astype(jnp.bfloat16)

    def chunk(b):
        begin = LEFT - W + b * DECIM * W
        d = nt(x_ref[:, begin:begin + (DECIM + 1) * W], ft)
        dec_ref[:, b * W:(b + 1) * W] = d
        put_mag(b, d)

    loaded = 0
    for b in range(1, nb):
        while loaded * seg < min((b + 1) * DECIM * W, raw_len):
            loads[loaded].wait()
            loaded += 1
        chunk(b)

    @pl.when(t > 0)
    def _():
        to_right.wait_recv()

    @pl.when(t < T - 1)
    def _():
        to_left.wait_recv()

    chunk(0)
    before = nt(x_ref[:, 0:LEFT], ft[:, 3 * W:5 * W])
    keep = (t > 0) & (lax.broadcasted_iota(jnp.int32, (rows, W), 1) >= W - HALF_WIN)
    put_mag(-1, jnp.where(keep, before, 0.0))
    after = nt(x_ref[:, LEFT + raw_len - W:LEFT + raw_len + RIGHT], ft[:, 0:2 * W])
    keep = (t < T - 1) & (lax.broadcasted_iota(jnp.int32, (rows, W), 1) < HALF_WIN)
    put_mag(nb, jnp.where(keep, after, 0.0))

    span = lax.broadcasted_iota(jnp.int32, (2 * W, 4 * W), 1) - W - lax.broadcasted_iota(
        jnp.int32, (2 * W, 4 * W), 0
    )
    band = jnp.where((span >= -HALF_WIN) & (span <= HALF_WIN), 1.0, 0.0).astype(jnp.bfloat16)
    mine = W + t * dec_len

    pr = lax.broadcasted_iota(jnp.int32, (T * SLAB, rows), 0)
    pc = lax.broadcasted_iota(jnp.int32, (T * SLAB, rows), 1)
    picks = jnp.zeros((T * SLAB, rows), jnp.float32)
    for g in range(T):
        for step in range(STEPS):
            for p in range(step_len):
                local = src_ref[step, g * step_len + p] - c * rows
                hit = (pr == g * SLAB + step * step_len + p) & (pc == local)
                picks = jnp.where(hit, 1.0, picks)
    picks = picks.astype(jnp.bfloat16)

    for p in range(nb // 2):
        cols = slice(2 * p * W, (2 * p + 4) * W)
        sums = nt(hi_ref[:, cols], band) + nt(lo_ref[:, cols], band)
        level = sums / (2 * HALF_WIN + 1) + 1e-05
        w = (dec_ref[:, 2 * p * W:2 * (p + 1) * W] / level).astype(jnp.bfloat16)
        white_ref[:, pl.ds(aligned(mine + 2 * p * W), 2 * W)] = w
        rows_of = jnp.dot(picks, w, preferred_element_type=jnp.float32)
        for g in range(T):
            part = rows_of[g * SLAB:(g + 1) * SLAB]
            send1[g * half + p] = jnp.concatenate(
                [part[:, :W], part[:, W:]], axis=0
            ).astype(jnp.bfloat16)

    def first(k, go):
        g, i = k // half, lax.rem(k, half)
        dest = t * half + i
        self_hit = (dest == c) & (g == t)
        remote = pltpu.make_async_remote_copy(
            src_ref=send1.at[k], dst_ref=recv1.at[c],
            send_sem=s1_sem.at[k], recv_sem=r1_sem,
            device_id=(dest, g), device_id_type=MESH,
        )

        @pl.when(jnp.logical_not(self_hit))
        def _():
            if go:
                remote.start()
            else:
                remote.wait_send()

        if go:
            @pl.when(self_hit)
            def _():
                pltpu.make_async_copy(send1.at[k], recv1.at[c], r1_sem).start()

    def each(count, body):
        def step(i, _):
            body(i)
            return 0
        lax.fori_loop(0, count, step, 0)

    each(T * half, lambda k: first(k, True))

    piece = dec_len // PIECES

    def bulk(d, i):
        cols = pl.ds(aligned(mine + i * piece), piece)
        return pltpu.make_async_remote_copy(
            src_ref=white_ref.at[:, cols], dst_ref=white_ref.at[:, cols],
            send_sem=bulk_send.at[d - 1, i], recv_sem=bulk_recv.at[d - 1, i],
            device_id=(c, lax.rem(t + d, T)), device_id_type=MESH,
        )

    for d in range(1, T):
        for i in range(PIECES):
            bulk(d, i).start()

    pltpu.make_async_copy(recv1, recv1, r1_sem).wait()
    summed = recv1[0].astype(jnp.float32)
    for j in range(1, C):
        summed = summed + recv1[j].astype(jnp.float32)
    send1[T * half] = summed.astype(jnp.bfloat16)

    def second(d):
        return pltpu.make_async_remote_copy(
            src_ref=send1.at[T * half], dst_ref=recv2.at[c],
            send_sem=s2_sem.at[d], recv_sem=r2_sem,
            device_id=(lax.rem(c + d + 1, C), t), device_id_type=MESH,
        )

    each(C - 1, lambda d: second(d).start())
    pltpu.make_async_copy(send1.at[T * half], recv2.at[c], r2_sem).start()
    pltpu.make_async_copy(recv2, recv2, r2_sem).wait()

    ahead = lane_id >= row_id
    main = ns * W
    gref[main:main + 16, 0:W] = jnp.zeros((16, W), jnp.bfloat16)
    for s in range(ns):
        def build(j, prev):
            x = recv2[j].astype(jnp.float32)
            for h in range(2):
                now = pltpu.roll(
                    jnp.broadcast_to(x[h * SLAB + s:h * SLAB + s + 1, :], (W, W)),
                    0, 1, stride=1, stride_axis=0,
                )
                gref[s * W:(s + 1) * W, pl.ds(aligned((2 * j + h) * W), W)] = jnp.where(
                    ahead, now, prev
                ).astype(jnp.bfloat16)
                if s == 0:
                    slab = x[h * SLAB:(h + 1) * SLAB]
                    gref[main:main + 16, pl.ds(aligned((2 * j + h + 1) * W), W)] = (
                        jnp.concatenate([slab, slab], axis=0).astype(jnp.bfloat16)
                    )
                prev = now
            return prev

        last = lax.fori_loop(0, C, build, jnp.zeros((W, W), jnp.float32))
        gref[s * W:(s + 1) * W, total:total + W] = jnp.where(ahead, 0.0, last).astype(
            jnp.bfloat16
        )

    def products(a, count):
        both = jnp.concatenate(
            [
                white_ref[:, pl.ds(aligned(a * W), count * W)],
                white_ref[:, pl.ds(aligned(a * W + W), count * W)],
            ],
            axis=0,
        )
        return nt(gref[:, pl.ds(aligned(a * W), count * W)], both)

    acc_ref[...] = products(t * nb + 1, nb - 1)
    step_chunks = nb // PIECES
    for d in range(1, T):
        b = lax.rem(t + T - d, T)
        for i in range(PIECES):
            bulk_in = pltpu.make_async_copy(
                white_ref.at[:, pl.ds(aligned(W + b * dec_len + i * piece), piece)],
                white_ref.at[:, pl.ds(aligned(W + b * dec_len + i * piece), piece)],
                bulk_recv.at[d - 1, i],
            )
            bulk_in.wait()
            skip = 1 if i == 0 else 0
            acc_ref[...] += products(b * nb + i * step_chunks + skip, step_chunks - skip)
    seams = [q * nb * W for q in range(T + 1)]
    both = jnp.concatenate(
        [
            jnp.concatenate([white_ref[:, q:q + W] for q in seams], axis=1),
            jnp.concatenate([white_ref[:, q + W:q + 2 * W] for q in seams], axis=1),
        ],
        axis=0,
    )
    acc_ref[...] += nt(jnp.concatenate([gref[:, q:q + W] for q in seams], axis=1), both)

    for s in range(ns):
        step, p = s // step_len, s % step_len
        out_ref[step, p, 0:W, :] = acc_ref[s * W:(s + 1) * W, 0:W] * scale
        out_ref[step, p, W:2 * W, :] = acc_ref[s * W:(s + 1) * W, W:2 * W] * scale
        out_ref[step, p, 2 * W:2 * W + 1, :] = acc_ref[main + s:main + s + 1, W:2 * W] * scale

    @pl.when(t < T - 1)
    def _():
        to_right.wait_send()

    @pl.when(t > 0)
    def _():
        to_left.wait_send()

    each(T * half, lambda k: first(k, False))
    each(C - 1, lambda d: second(d).wait_send())
    for d in range(1, T):
        for i in range(PIECES):
            bulk(d, i).wait_send()


def per_device(C, T, raw_strain, fir_taps, sources):
    rows, raw_len = raw_strain.shape
    dec_len = raw_len // DECIM
    nb = dec_len // W
    half = nb * C // (T * nb)
    step_len = sources.shape[1] // T
    ns = STEPS * step_len
    total = T * dec_len
    bf, f32 = jnp.bfloat16, jnp.float32
    return pl.pallas_call(
        functools.partial(kernel, C, T, 1.0 / math.sqrt(total)),
        out_shape=jax.ShapeDtypeStruct((STEPS, step_len, LAGS, rows), f32),
        in_specs=[
            pl.BlockSpec(memory_space=pl.ANY),
            pl.BlockSpec(memory_space=pltpu.VMEM),
            pl.BlockSpec(memory_space=pltpu.SMEM),
        ],
        out_specs=pl.BlockSpec(memory_space=pltpu.VMEM),
        scratch_shapes=[
            pltpu.VMEM((rows, LEFT + raw_len + RIGHT), bf),
            pltpu.VMEM((rows, dec_len), f32),
            pltpu.VMEM((rows, dec_len + 2 * W), bf),
            pltpu.VMEM((rows, dec_len + 2 * W), bf),
            pltpu.VMEM((rows, total + 2 * W), bf),
            pltpu.VMEM((T * half + 1, 16, W), bf),
            pltpu.VMEM((C, 16, W), bf),
            pltpu.VMEM((C, 16, W), bf),
            pltpu.VMEM((ns * W + 16, total + W), bf),
            pltpu.VMEM((ns * W + 16, 2 * W), f32),
            pltpu.SemaphoreType.DMA((PIECES,)),
            pltpu.SemaphoreType.DMA((2,)),
            pltpu.SemaphoreType.DMA((2,)),
            pltpu.SemaphoreType.DMA((T * half,)),
            pltpu.SemaphoreType.DMA,
            pltpu.SemaphoreType.DMA((C,)),
            pltpu.SemaphoreType.DMA,
            pltpu.SemaphoreType.DMA,
            pltpu.SemaphoreType.DMA((T, PIECES)),
            pltpu.SemaphoreType.DMA((T, PIECES)),
        ],
        compiler_params=pltpu.CompilerParams(
            collective_id=0, has_side_effects=True, vmem_limit_bytes=40 * 1024 * 1024
        ),
    )(raw_strain, fir_taps.reshape(1, TAPS), sources)


def solution(mesh):
    C, T = mesh.shape["chan"], mesh.shape["tm"]
    return jax.shard_map(
        functools.partial(per_device, C, T),
        mesh=mesh,
        in_specs=(P("chan", "tm"), P(), P()),
        out_specs=P(None, "tm", None, "chan"),
        check_vma=False,
    )
```

time: 402 us -> 46.6 us (0.12)
  local copies, waits for them, and re-layouts: 221 us -> 4.17 us
  waiting for transfers between devices: 63.8 us -> 0 us
  blocking collectives: 60.9 us -> 0 us
  Pallas kernels: 0 us -> 42.2 us
  starting transfers between devices: 16.7 us -> 0 us
  between operations: 14.4 us -> 0.01 us
  other arithmetic: 11.8 us -> 0 us
  matrix products: 9.57 us -> 0 us
    dynamic_update_slice x32 -> x0, local copies, waits for them, and re-layouts: 82.6 us -> none  [lag_products(): return lax.map(single, extended_traces)]
    rev x16 -> x0, local copies, waits for them, and re-layouts: 63.6 us -> none  [single(): toeplitz = tiled[::-1, :length]]
    psum x1 -> x0, blocking collectives: 60.9 us -> none  [per_device(): lax.psum(jnp.dot(picks.astype(jnp.bfloat16), white, preferred_element_typ...]
    unnamed x2 -> x0, waiting for transfers between devices: 59.8 us -> none
    pallas_call x0 -> x1, Pallas kernels: none -> 42.2 us  [per_device(): pl.pallas_call(functools.partial(kernel, C, T, 1.0 / math.sqrt(total)), o...]
    reshape x18 -> x0, local copies, waits for them, and re-layouts: 34.6 us -> none  [the longest x16 33.7 us: single(): jnp.tile(trace, LAGS + 1)[:LAGS * (width + 1)].reshape(LAGS, width + 1)]
    another operation x34 -> x0, local copies, waits for them, and re-layouts: 25.5 us -> none  [the longest x32 23.4 us: single(): jnp.tile(trace, LAGS + 1)[:LAGS * (width + 1)].reshape(LAGS, width + 1)]
    ppermute x7 -> x0, starting transfers between devices: 16.7 us -> none  [the longest x3 7.76 us: padded_2(): before = lax.ppermute(last, axis, up)]
  transfers between devices with their start and end apart: 8 -> 0, of which waited for: 2 -> 0; matrix products, arithmetic and copies ran while one was open for 29% -> 0% of each run, Pallas kernels for 0% -> 0%
where the time goes in v1:
time: 46.6 us; the launch traced here: 46.4 us
  Pallas kernels  42.2 us (91%)
  local copies, waits for them, and re-layouts  4.17 us (9%)
    pallas_call x1, Pallas kernels, per_device(): pl.pallas_call(functools.partial(kernel, C, T, 1.0 / math.sqrt(total)), o...  42.2 us
    unnamed x6, local copies, waits for them, and re-layouts  2.92 us
    pallas_call x1, local copies, waits for them, and re-layouts, per_device(): pl.pallas_call(functools.partial(kernel, C, T, 1.0 / math.sqrt(total)), o...  1.24 us

profile of v1, /device:TPU:0, one launch (start us, length us, event | category | flops | bytes accessed | tf_op | source)
XLA Modules:
  0.0 46.4 jit_solution(1785804519629061005)
XLA Ops:
  0.0 0.0 copy-start
  0.0 1.6 %copy-done = bf16[128,8192]{1,0:T(8,128)(2,1)S(1)} copy-done((bf16[128,8192]{1,0:T(8,128)(2,1)S(1)}, bf16[128,8192]{1,0:T(8,128)(2,1)}, u32[]{:S(2)}) %copy-start) | copy-done | bytes 2097176
  1.6 0.0 copy-start.1
  1.6 0.7 %copy-done.1 = s32[2,8]{1,0:T(2,128)S(1)} copy-done((s32[2,8]{1,0:T(2,128)S(1)}, s32[2,8]{1,0:T(2,128)}, u32[]{:S(2)}) %copy-start.1) | copy-done | bytes 88
  2.3 0.0 copy-start.2
  2.3 0.7 %copy-done.2 = bf16[64]{0:T(256)(128)(2,1)S(1)} copy-done((bf16[64]{0:T(256)(128)(2,1)S(1)}, bf16[64]{0:T(256)(128)(2,1)}, u32[]{:S(2)}) %copy-start.2) | copy-done | bytes 152
  2.9 42.2 %shard_map.37 = f32[2,4,257,128]{3,2,1,0:T(8,128)S(1)} custom-call(bf16[128,8192]{1,0:T(8,128)(2,1)S(1)} %copy-done, bf16[1,64]{1,0:T(2,128)(2,1)S(1)} %bitcast.1, s32[2,8]{1,0:T(2,128)S(1)} %copy-done.1), custom_call_target="tpu_custom_call" | custom-call | tf_op jit(solution)/shard_map/pallas_call | solution.py:344
  45.2 1.2 %copy.4 = f32[2,4,257,128]{3,1,2,0:T(4,128)} copy(f32[2,4,257,128]{3,2,1,0:T(8,128)S(1)} %shard_map.37) | data formatting | bytes 2105344 | tf_op jit(solution)/shard_map/pallas_call | solution.py:344
Async XLA Ops:
  0.0 1.6 %copy-start = (bf16[128,8192]{1,0:T(8,128)(2,1)S(1)}, bf16[128,8192]{1,0:T(8,128)(2,1)}, u32[]{:S(2)}) copy-start(bf16[128,8192]{1,0:T(8,128)(2,1)} %raw_ref.1) | copy-start | bytes 6291460
  1.6 0.7 %copy-start.1 = (s32[2,8]{1,0:T(2,128)S(1)}, s32[2,8]{1,0:T(2,128)}, u32[]{:S(2)}) copy-start(s32[2,8]{1,0:T(2,128)} %src_ref.1) | copy-start | bytes 196
  2.3 0.7 %copy-start.2 = (bf16[64]{0:T(256)(128)(2,1)S(1)}, bf16[64]{0:T(256)(128)(2,1)}, u32[]{:S(2)}) copy-start(bf16[64]{0:T(256)(128)(2,1)} %param.4) | copy-start | bytes 388

commit v2 on v1

v2 whole, which is shorter than its diff:
```python
import functools
import math

import jax
import jax.numpy as jnp
from jax import lax
from jax.experimental import pallas as pl
from jax.experimental.pallas import tpu as pltpu
from jax.sharding import PartitionSpec as P

TAPS = 64
DECIM = 4
HALF_WIN = 32
LAGS = 257
HALF_LAG = 128
STEPS = 2
W = 128
SLAB = 8
PIECES = 4
LEFT = 256
RIGHT = 128
MESH = pl.DeviceIdType.MESH


def nt(a, b):
    return lax.dot_general(
        a, b, (((1,), (1,)), ((), ())), preferred_element_type=jnp.float32
    )


def aligned(x):
    return pl.multiple_of(x, W)


def kernel(
    C, T, scale,
    raw_ref, taps_hbm, src_hbm, out_ref,
    taps_ref, src_ref, praw_ref, rep_ref, x_ref, dec_ref, hi_ref, lo_ref, white_ref, send1, recv1, recv2, gref, acc_ref,
    small_sem, load_sem, halo_send, halo_recv, s1_sem, r1_sem, s2_sem, r2_sem, own_sem, bulk_send, bulk_recv,
):
    c = lax.axis_index("chan")
    t = lax.axis_index("tm")
    N = C * T
    rows, raw_len = raw_ref.shape
    dec_len = raw_len // DECIM
    nb = dec_len // W
    per_dev = (T * nb) // C
    half = nb // per_dev
    step_len = src_hbm.shape[1] // T
    ns = STEPS * step_len
    me = c * T + t

    barrier = pltpu.get_barrier_semaphore()

    def greet(d, _):
        other = lax.rem(me + d, N)
        pl.semaphore_signal(
            barrier, inc=1, device_id=(other // T, lax.rem(other, T)), device_id_type=MESH
        )
        return 0

    lax.fori_loop(1, N, greet, 0)

    small = [
        pltpu.make_async_copy(taps_hbm, taps_ref, small_sem.at[0]),
        pltpu.make_async_copy(src_hbm, src_ref, small_sem.at[1]),
    ]
    for copy in small:
        copy.start()
    seg = raw_len // PIECES
    loads = []
    for i in range(PIECES):
        load = pltpu.make_async_copy(
            raw_ref.at[:, pl.ds(i * seg, seg)],
            x_ref.at[:, pl.ds(LEFT + i * seg, seg)],
            load_sem.at[i],
        )
        load.start()
        loads.append(load)

    for copy in small:
        copy.wait()

    taps = jnp.broadcast_to(taps_ref[...], (16, TAPS))
    place = lax.broadcasted_iota(jnp.int32, (TAPS, W), 1) == lax.rem(
        W - lax.broadcasted_iota(jnp.int32, (TAPS, W), 0), W
    )
    base = jnp.dot(
        taps, place.astype(jnp.float32).astype(jnp.bfloat16), preferred_element_type=jnp.float32
    )
    rolled = pltpu.roll(
        jnp.broadcast_to(base[0:1, :], (W, W)), 0, 1, stride=DECIM, stride_axis=0
    )
    row_id = lax.broadcasted_iota(jnp.int32, (W, W), 0)
    lane_id = lax.broadcasted_iota(jnp.int32, (W, W), 1)
    fts = []
    for jc in range(DECIM + 1):
        k = DECIM * row_id + W - W * jc - lane_id
        fts.append(jnp.where((k >= 0) & (k < W), rolled, 0.0).astype(jnp.bfloat16))
    ft = jnp.concatenate(fts, axis=1)

    pr = lax.broadcasted_iota(jnp.int32, (T * SLAB, rows), 0)
    pc = lax.broadcasted_iota(jnp.int32, (T * SLAB, rows), 1)
    picks = jnp.zeros((T * SLAB, rows), jnp.float32)
    for g in range(T):
        for step in range(STEPS):
            for p in range(step_len):
                local = src_ref[step, g * step_len + p] - c * rows
                hit = (pr == g * SLAB + step * step_len + p) & (pc == local)
                picks = jnp.where(hit, 1.0, picks)
    picks = picks.astype(jnp.bfloat16)

    pl.semaphore_wait(barrier, N - 1)

    to_right = pltpu.make_async_remote_copy(
        src_ref=raw_ref.at[:, pl.ds(raw_len - LEFT, LEFT)],
        dst_ref=x_ref.at[:, pl.ds(0, LEFT)],
        send_sem=halo_send.at[0], recv_sem=halo_recv.at[0],
        device_id=(c, lax.rem(t + 1, T)), device_id_type=MESH,
    )
    to_left = pltpu.make_async_remote_copy(
        src_ref=raw_ref.at[:, pl.ds(0, RIGHT)],
        dst_ref=x_ref.at[:, pl.ds(LEFT + raw_len, RIGHT)],
        send_sem=halo_send.at[1], recv_sem=halo_recv.at[1],
        device_id=(c, lax.rem(t + T - 1, T)), device_id_type=MESH,
    )

    @pl.when(t < T - 1)
    def _():
        to_right.start()

    @pl.when(t > 0)
    def _():
        to_left.start()

    @pl.when(t == 0)
    def _():
        x_ref[:, 0:LEFT] = jnp.zeros((rows, LEFT), jnp.bfloat16)

    @pl.when(t == T - 1)
    def _():
        x_ref[:, LEFT + raw_len:] = jnp.zeros((rows, RIGHT), jnp.bfloat16)

    total = T * dec_len
    white_ref[:, 0:W] = jnp.zeros((rows, W), jnp.bfloat16)
    white_ref[:, W + total:] = jnp.zeros((rows, W), jnp.bfloat16)

    def put_mag(b, d):
        mag = jnp.abs(d)
        hi = mag.astype(jnp.bfloat16)
        hi_ref[:, (b + 1) * W:(b + 2) * W] = hi
        lo_ref[:, (b + 1) * W:(b + 2) * W] = (mag - hi.astype(jnp.float32)).astype(jnp.bfloat16)

    def chunk(b):
        begin = LEFT - W + b * DECIM * W
        d = nt(x_ref[:, begin:begin + (DECIM + 1) * W], ft)
        dec_ref[:, b * W:(b + 1) * W] = d
        put_mag(b, d)

    def pick_raw(x):
        return jnp.dot(picks, x, preferred_element_type=jnp.float32).astype(jnp.bfloat16)

    lead = (DECIM + 1) * W
    many = T * SLAB
    praw_ref[:, 0:lead - LEFT] = jnp.zeros((many, lead - LEFT), jnp.bfloat16)
    praw_ref[:, lead + raw_len + RIGHT:] = jnp.zeros((many, DECIM * W - RIGHT), jnp.bfloat16)
    for i in range(PIECES):
        loads[i].wait()
        praw_ref[:, lead + i * seg:lead + (i + 1) * seg] = pick_raw(
            x_ref[:, LEFT + i * seg:LEFT + (i + 1) * seg]
        )
    for b in range(1, nb):
        chunk(b)

    @pl.when(t > 0)
    def _():
        to_right.wait_recv()

    @pl.when(t < T - 1)
    def _():
        to_left.wait_recv()

    praw_ref[:, lead - LEFT:lead] = pick_raw(x_ref[:, 0:LEFT])
    praw_ref[:, lead + raw_len:lead + raw_len + RIGHT] = pick_raw(x_ref[:, LEFT + raw_len:])
    picked = nt(
        jnp.concatenate(
            [praw_ref[:, b * DECIM * W:b * DECIM * W + lead] for b in range(nb + 2)], axis=0
        ),
        ft,
    )
    size = (nb + 2) * many
    pr = lax.broadcasted_iota(jnp.int32, (size, W), 0)
    pc = lax.broadcasted_iota(jnp.int32, (size, W), 1)
    inside = ((pr >= many) | ((t > 0) & (pc >= W - HALF_WIN))) & (
        (pr < size - many) | ((t < T - 1) & (pc < HALF_WIN))
    )
    mag = jnp.where(inside, jnp.abs(picked), 0.0)
    hi = mag.astype(jnp.bfloat16)
    lo = (mag - hi.astype(jnp.float32)).astype(jnp.bfloat16)
    wide = jnp.concatenate(
        [m[k * many:k * many + nb * many] for m in (hi, lo) for k in range(3)], axis=1
    )
    span = lax.broadcasted_iota(jnp.int32, (W, 3 * W), 1) - W - lax.broadcasted_iota(
        jnp.int32, (W, 3 * W), 0
    )
    band = jnp.where((span >= -HALF_WIN) & (span <= HALF_WIN), 1.0, 0.0).astype(jnp.bfloat16)
    level = nt(wide, jnp.concatenate([band, band], axis=1)) / (2 * HALF_WIN + 1) + 1e-05
    picked = picked[many:many + nb * many] / level
    for g in range(T):
        for i in range(half):
            send1[g * half + i] = jnp.concatenate(
                [
                    picked[q * many + g * SLAB:q * many + (g + 1) * SLAB]
                    for q in (2 * i, 2 * i + 1)
                ],
                axis=0,
            ).astype(jnp.bfloat16)

    def first(k, go):
        g, i = k // half, k % half
        dest = t * half + i
        self_hit = (dest == c) & (g == t)
        remote = pltpu.make_async_remote_copy(
            src_ref=send1.at[k], dst_ref=recv1.at[c],
            send_sem=s1_sem.at[k], recv_sem=r1_sem,
            device_id=(dest, g), device_id_type=MESH,
        )

        @pl.when(jnp.logical_not(self_hit))
        def _():
            if go:
                remote.start()
            else:
                remote.wait_send()

        if go:
            @pl.when(self_hit)
            def _():
                pltpu.make_async_copy(send1.at[k], recv1.at[c], r1_sem).start()

    def each(count, body):
        if count <= 16:
            for i in range(count):
                body(i)
            return

        def step(i, _):
            body(i)
            return 0

        lax.fori_loop(0, count, step, 0)

    each(T * half, lambda k: first(k, True))

    chunk(0)
    before = nt(x_ref[:, 0:LEFT], ft[:, 3 * W:5 * W])
    keep = (t > 0) & (lax.broadcasted_iota(jnp.int32, (rows, W), 1) >= W - HALF_WIN)
    put_mag(-1, jnp.where(keep, before, 0.0))
    after = nt(x_ref[:, LEFT + raw_len - W:LEFT + raw_len + RIGHT], ft[:, 0:2 * W])
    keep = (t < T - 1) & (lax.broadcasted_iota(jnp.int32, (rows, W), 1) < HALF_WIN)
    put_mag(nb, jnp.where(keep, after, 0.0))

    span = lax.broadcasted_iota(jnp.int32, (2 * W, 4 * W), 1) - W - lax.broadcasted_iota(
        jnp.int32, (2 * W, 4 * W), 0
    )
    band = jnp.where((span >= -HALF_WIN) & (span <= HALF_WIN), 1.0, 0.0).astype(jnp.bfloat16)
    mine = W + t * dec_len

    piece = dec_len // PIECES

    def bulk(d, i):
        cols = pl.ds(aligned(mine + i * piece), piece)
        return pltpu.make_async_remote_copy(
            src_ref=white_ref.at[:, cols], dst_ref=white_ref.at[:, cols],
            send_sem=bulk_send.at[d - 1, i], recv_sem=bulk_recv.at[d - 1, i],
            device_id=(c, lax.rem(t + d, T)), device_id_type=MESH,
        )

    for p in range(nb // 2):
        cols = slice(2 * p * W, (2 * p + 4) * W)
        sums = nt(hi_ref[:, cols], band) + nt(lo_ref[:, cols], band)
        level = sums / (2 * HALF_WIN + 1) + 1e-05
        w = (dec_ref[:, 2 * p * W:2 * (p + 1) * W] / level).astype(jnp.bfloat16)
        white_ref[:, pl.ds(aligned(mine + 2 * p * W), 2 * W)] = w
        if (2 * p + 2) * W % piece == 0:
            for d in range(1, T):
                bulk(d, (2 * p + 2) * W // piece - 1).start()

    pltpu.make_async_copy(recv1, recv1, r1_sem).wait()
    summed = recv1[0].astype(jnp.float32)
    for j in range(1, C):
        summed = summed + recv1[j].astype(jnp.float32)
    send1[T * half] = summed.astype(jnp.bfloat16)

    def second(d):
        return pltpu.make_async_remote_copy(
            src_ref=send1.at[T * half], dst_ref=recv2.at[c],
            send_sem=s2_sem.at[d], recv_sem=r2_sem,
            device_id=(lax.rem(c + d + 1, C), t), device_id_type=MESH,
        )

    each(C - 1, lambda d: second(d).start())
    pltpu.make_async_copy(send1.at[T * half], recv2.at[c], r2_sem).start()
    pltpu.make_async_copy(recv2, recv2, r2_sem).wait()

    group = 16 // step_len
    main = ns * W
    gathered = jnp.concatenate([recv2[j] for j in range(C)], axis=1)
    spread_row = lax.broadcasted_iota(jnp.int32, (2 * STEPS * 16, 16), 0)
    spread_col = lax.broadcasted_iota(jnp.int32, (2 * STEPS * 16, 16), 1)
    wanted = (spread_row // (STEPS * 16)) * SLAB + (spread_row // 16 % STEPS) * step_len + (
        spread_row % step_len
    )
    spread = jnp.where(spread_col == wanted, 1.0, 0.0).astype(jnp.bfloat16)
    rep_ref[...] = jnp.dot(spread, gathered, preferred_element_type=jnp.float32).astype(
        jnp.bfloat16
    )
    slabs = gathered.astype(jnp.float32)
    gref[main:main + 16, 0:W] = jnp.zeros((16, W), jnp.bfloat16)
    for q in range(2 * C):
        slab = slabs[q % 2 * SLAB:(q % 2 + 1) * SLAB, q // 2 * W:(q // 2 + 1) * W]
        gref[main:main + 16, (q + 1) * W:(q + 2) * W] = jnp.concatenate(
            [slab, slab], axis=0
        ).astype(jnp.bfloat16)
    low = (lax.broadcasted_iota(jnp.int32, (16, W), 0) // step_len)
    low_lane = (lax.broadcasted_iota(jnp.int32, (16, W), 1) - low).astype(jnp.int16)
    low = low.astype(jnp.int16)
    tiles = W // group
    for step in range(STEPS):
        first_row = step * step_len * W

        def tile(a, now, prev, column):
            gref[first_row + a * 16:first_row + (a + 1) * 16, pl.ds(column, W)] = jnp.where(
                low_lane >= a * group, now, prev
            )

        def build(j, prev):
            for h in range(2):
                top = (h * STEPS + step) * 16
                x = rep_ref[top:top + 16, pl.ds(aligned(j * W), W)]
                start = x
                for k in range(1, group):
                    start = jnp.where(low == k, pltpu.roll(x, k, 1), start)
                out = []
                for a in range(tiles):
                    now = pltpu.roll(start, a * group, 1) if a else start
                    tile(a, now, prev[a], aligned((2 * j + h) * W))
                    out.append(now)
                prev = tuple(out)
            return prev

        last = lax.fori_loop(0, C, build, (jnp.zeros((16, W), jnp.bfloat16),) * tiles)
        for a in range(tiles):
            tile(a, jnp.zeros((16, W), jnp.bfloat16), last[a], total)

    def products(a, count):
        both = jnp.concatenate(
            [
                white_ref[:, pl.ds(aligned(a * W), count * W)],
                white_ref[:, pl.ds(aligned(a * W + W), count * W)],
            ],
            axis=0,
        )
        return nt(gref[:, pl.ds(aligned(a * W), count * W)], both)

    acc_ref[...] = products(t * nb + 1, nb - 1)
    step_chunks = nb // PIECES
    for d in range(1, T):
        b = lax.rem(t + T - d, T)
        for i in range(PIECES):
            bulk_in = pltpu.make_async_copy(
                white_ref.at[:, pl.ds(aligned(W + b * dec_len + i * piece), piece)],
                white_ref.at[:, pl.ds(aligned(W + b * dec_len + i * piece), piece)],
                bulk_recv.at[d - 1, i],
            )
            bulk_in.wait()
            skip = 1 if i == 0 else 0
            acc_ref[...] += products(b * nb + i * step_chunks + skip, step_chunks - skip)
    seams = [q * nb * W for q in range(T + 1)]
    both = jnp.concatenate(
        [
            jnp.concatenate([white_ref[:, q:q + W] for q in seams], axis=1),
            jnp.concatenate([white_ref[:, q + W:q + 2 * W] for q in seams], axis=1),
        ],
        axis=0,
    )
    acc_ref[...] += nt(jnp.concatenate([gref[:, q:q + W] for q in seams], axis=1), both)

    span = step_len * W
    for step in range(STEPS):
        at, to = step * span, step * step_len * LAGS
        out_ref[to:to + span, :] = acc_ref[at:at + span, 0:W] * scale
        out_ref[to + span:to + 2 * span, :] = acc_ref[at:at + span, W:2 * W] * scale
        extra = main + step * step_len
        out_ref[to + 2 * span:to + 2 * span + step_len, :] = (
            acc_ref[extra:extra + step_len, W:2 * W] * scale
        )

    @pl.when(t < T - 1)
    def _():
        to_right.wait_send()

    @pl.when(t > 0)
    def _():
        to_left.wait_send()

    each(T * half, lambda k: first(k, False))
    each(C - 1, lambda d: second(d).wait_send())
    for d in range(1, T):
        for i in range(PIECES):
            bulk(d, i).wait_send()


def per_device(C, T, raw_strain, fir_taps, sources):
    rows, raw_len = raw_strain.shape
    dec_len = raw_len // DECIM
    nb = dec_len // W
    half = nb * C // (T * nb)
    step_len = sources.shape[1] // T
    ns = STEPS * step_len
    total = T * dec_len
    bf, f32 = jnp.bfloat16, jnp.float32
    flat = pl.pallas_call(
        functools.partial(kernel, C, T, 1.0 / math.sqrt(total)),
        out_shape=jax.ShapeDtypeStruct((STEPS * LAGS * step_len, rows), f32),
        in_specs=[
            pl.BlockSpec(memory_space=pltpu.HBM),
            pl.BlockSpec(memory_space=pltpu.HBM),
            pl.BlockSpec(memory_space=pltpu.HBM),
        ],
        out_specs=pl.BlockSpec(memory_space=pltpu.VMEM),
        scratch_shapes=[
            pltpu.VMEM((1, TAPS), bf),
            pltpu.SMEM(sources.shape, jnp.int32),
            pltpu.VMEM((T * SLAB, raw_len + (2 * DECIM + 1) * W), bf),
            pltpu.VMEM((2 * STEPS * 16, C * W), bf),
            pltpu.VMEM((rows, LEFT + raw_len + RIGHT), bf),
            pltpu.VMEM((rows, dec_len), f32),
            pltpu.VMEM((rows, dec_len + 2 * W), bf),
            pltpu.VMEM((rows, dec_len + 2 * W), bf),
            pltpu.VMEM((rows, total + 2 * W), bf),
            pltpu.VMEM((T * half + 1, 16, W), bf),
            pltpu.VMEM((C, 16, W), bf),
            pltpu.VMEM((C, 16, W), bf),
            pltpu.VMEM((ns * W + 16, total + W), bf),
            pltpu.VMEM((ns * W + 16, 2 * W), f32),
            pltpu.SemaphoreType.DMA((2,)),
            pltpu.SemaphoreType.DMA((PIECES,)),
            pltpu.SemaphoreType.DMA((2,)),
            pltpu.SemaphoreType.DMA((2,)),
            pltpu.SemaphoreType.DMA((T * half,)),
            pltpu.SemaphoreType.DMA,
            pltpu.SemaphoreType.DMA((C,)),
            pltpu.SemaphoreType.DMA,
            pltpu.SemaphoreType.DMA,
            pltpu.SemaphoreType.DMA((T, PIECES)),
            pltpu.SemaphoreType.DMA((T, PIECES)),
        ],
        compiler_params=pltpu.CompilerParams(
            collective_id=0, has_side_effects=True, vmem_limit_bytes=62 * 1024 * 1024
        ),
    )(raw_strain, fir_taps.reshape(1, TAPS), sources)
    return jnp.swapaxes(flat.reshape(STEPS, LAGS, step_len, rows), 1, 2)


def solution(mesh):
    C, T = mesh.shape["chan"], mesh.shape["tm"]
    return jax.shard_map(
        functools.partial(per_device, C, T),
        mesh=mesh,
        in_specs=(P("chan", "tm"), P(), P()),
        out_specs=P(None, "tm", None, "chan"),
        check_vma=False,
    )
```

time: 46.6 us -> 35.9 us (0.77)
  Pallas kernels: 42.2 us -> 33.5 us
  local copies, waits for them, and re-layouts: 4.17 us -> 2.27 us
    pallas_call x1, Pallas kernels: 42.2 us -> 33.5 us  [per_device(): pl.pallas_call(functools.partial(kernel, C, T, 1.0 / math.sqrt(total)), o...]
    pallas_call x1 -> x0, local copies, waits for them, and re-layouts: 1.24 us -> none  [per_device(): pl.pallas_call(functools.partial(kernel, C, T, 1.0 / math.sqrt(total)), o...]
    unnamed x6 -> x1, local copies, waits for them, and re-layouts: 2.92 us -> 2.27 us
where the time goes in v2:
time: 35.9 us; the launch traced here: 35.7 us
  Pallas kernels  33.5 us (93%)
  local copies, waits for them, and re-layouts  2.27 us (6%)
    pallas_call x1, Pallas kernels, per_device(): pl.pallas_call(functools.partial(kernel, C, T, 1.0 / math.sqrt(total)), o...  33.5 us
    unnamed x1, local copies, waits for them, and re-layouts  2.27 us

profile of v2, /device:TPU:0, one launch (start us, length us, event | category | flops | bytes accessed | tf_op | source)
XLA Modules:
  0.0 35.7 jit_solution(4018698623130816314)
XLA Ops:
  0.0 33.5 %shard_map.37 = f32[2056,128]{1,0:T(8,128)} custom-call(bf16[128,8192]{1,0:T(8,128)(2,1)} %raw_ref.1, bf16[1,64]{1,0:T(2,128)(2,1)} %bitcast.5, s32[2,8]{1,0:T(2,128)} %src_hbm.1), custom_call_target="tpu_custom_call" | custom-call | tf_op jit(solution)/shard_map/pallas_call | solution.py:423
  33.5 2.3 %copy.5 = f32[2,4,257,128]{3,1,2,0:T(4,128)} copy(f32[2,4,257,128]{3,1,2,0:T(4,128)} %bitcast.4) | data formatting | bytes 2105344

commit v3 on v2

--- a/solution.py
+++ b/solution.py
@@ -422,7 +422,7 @@
     bf, f32 = jnp.bfloat16, jnp.float32
     flat = pl.pallas_call(
         functools.partial(kernel, C, T, 1.0 / math.sqrt(total)),
-        out_shape=jax.ShapeDtypeStruct((STEPS * LAGS * step_len, rows), f32),
+        out_shape=pltpu.VMEM((STEPS * LAGS * step_len, rows), f32),
         in_specs=[
             pl.BlockSpec(memory_space=pltpu.HBM),
             pl.BlockSpec(memory_space=pltpu.HBM),

time: 35.9 us -> 33.6 us (0.936)
  local copies, waits for them, and re-layouts: 2.27 us -> 0.97 us
  Pallas kernels: 33.5 us -> 32.5 us
    unnamed x1, local copies, waits for them, and re-layouts: 2.27 us -> 0.97 us
    pallas_call x1, Pallas kernels: 33.5 us -> 32.5 us  [per_device(): pl.pallas_call(functools.partial(kernel, C, T, 1.0 / math.sqrt(total)), o...]
where the time goes in v3:
time: 33.6 us; the launch traced here: 33.4 us
  Pallas kernels  32.5 us (97%)
  local copies, waits for them, and re-layouts  0.97 us (3%)
    pallas_call x1, Pallas kernels, per_device(): pl.pallas_call(functools.partial(kernel, C, T, 1.0 / math.sqrt(total)), o...  32.5 us
    unnamed x1, local copies, waits for them, and re-layouts  0.97 us

profile of v3, /device:TPU:0, one launch (start us, length us, event | category | flops | bytes accessed | tf_op | source)
XLA Modules:
  0.0 33.4 jit_solution(12982286405405561307)
XLA Ops:
  0.0 32.5 %shard_map.37 = f32[2056,128]{1,0:T(8,128)S(1)} custom-call(bf16[128,8192]{1,0:T(8,128)(2,1)} %raw_ref.1, bf16[1,64]{1,0:T(2,128)(2,1)} %bitcast.5, s32[2,8]{1,0:T(2,128)} %src_hbm.1), custom_call_target="tpu_custom_call" | custom-call | tf_op jit(solution)/shard_map/pallas_call | solution.py:423
  32.5 1.0 %copy.5 = f32[2,4,257,128]{3,1,2,0:T(4,128)} copy(f32[2,4,257,128]{3,1,2,0:T(4,128)S(1)} %bitcast.4) | data formatting | bytes 2105344
